TPU v7x, 256 devices: a whole 4x4x8 slice. The times are simulated.
256 devices in a mesh: stretch: 4 (over z_hi), space: 64 (over x, y, z_lo, core).
Axes of the slice: x: 4, y: 4, z: 8 (z_hi: 4, z_lo: 2; z = z_hi * 2 + z_lo), core: 2. Of those that a mesh axis runs over, the one named last changes fastest.
Arguments:
- queries: bfloat16 [4, 1024, 3072], P('stretch', 'space'), may hold values from -8 to 8
- stretch_keys: bfloat16 [4, 1024, 3072], P('stretch', 'space'), may hold values from -4 to 4
- stretch_values: bfloat16 [4, 1024, 3072], P('stretch', 'space'), may hold values from -6 to 6
- cache_keys: bfloat16 [32, 1024, 3072], P('stretch', 'space'), may hold values from -4 to 4
- cache_values: bfloat16 [32, 1024, 3072], P('stretch', 'space'), may hold values from -6 to 6
- block_list: int32 [4, 16], replicated, may hold values from 0 to 31, as said below
- list_len: int32 [4], replicated, may hold values from 4 to 16
- tok_count: int32 [4], replicated, may hold values from 512 to 1024, as said below
- noise_levels: int32 [4], replicated, may hold values from 0 to 47
- gate_table: float32 [48, 3072], replicated, may hold values from 0.1 to 1.9
Outputs:
- shifted: bfloat16 [4, 1024, 3072], P('stretch', 'space')
Inputs may be any that keep to these rules, and one draw needn't show every extreme that they name: `block_list`: stretch c's list names list_len[c] distinct blocks; the owner of block b is b // 8; at most 4 of one list's blocks have one owner, and every list has exactly 4 from some owner; in every draw one stretch's list is full, with 4 blocks from every owner, and another stretch's list holds exactly 4 blocks; entries from list_len[c] on are 0. `tok_count`: some stretch has all 1024 slots valid in every draw.
All inputs are finite; a program needn't handle non-finite values.
Results may differ from a plain program's by a relative error of at most 0.025.
Values may be sent and summed in bfloat16 or wider, within the bound.
A program may use at most 128 MiB of HBM per device.

v0:
```python
import math

import jax
import jax.numpy as jnp
from jax import lax
from jax.sharding import PartitionSpec as P

HEADS = 24
HEAD_DIM = 128
PER_SRC = 4


MASKED_SCORE = -1e30


def passed_along(value, axis, steps):
    count = lax.axis_size(axis)
    pairs = [(source, (source + steps) % count) for source in range(count)]
    return lax.ppermute(value, axis, pairs)


def flash_update(carry_state, key_rows, value_rows, keep_mask, every_query, score_scale):
    run_max, run_sum, accumulated = carry_state
    scores = (
        jnp.einsum("khd,qhd->hkq", key_rows, every_query, preferred_element_type=jnp.float32)
        * score_scale
    )
    scores = jnp.where(keep_mask[None, :, None], scores, MASKED_SCORE)
    new_max = jnp.maximum(run_max, jnp.max(scores, axis=1))
    weights = jnp.where(keep_mask[None, :, None], jnp.exp(scores - new_max[:, None, :]), 0.0)
    factor = jnp.exp(run_max - new_max)
    new_sum = run_sum * factor + jnp.sum(weights, axis=1)
    update = jnp.einsum(
        "hkq,khd->qhd", weights.astype(jnp.bfloat16), value_rows, preferred_element_type=jnp.float32
    )
    new_acc = accumulated * jnp.transpose(factor)[:, :, None] + update
    return (new_max, new_sum, new_acc)


def shards(
    queries,
    stretch_keys,
    stretch_values,
    cache_keys,
    cache_values,
    block_list,
    list_len,
    tok_count,
    noise_levels,
    gate_table,
):
    stretch_id = lax.axis_index("stretch")
    space_id = lax.axis_index("space")
    local_tok = queries.shape[1]
    features = queries.shape[2]
    score_scale = 1.0 / math.sqrt(HEAD_DIM)
    gathered = lax.all_gather(queries, "space", axis=1, tiled=True)
    query_span = gathered.shape[1]
    every_query = gathered.reshape(query_span, HEADS, HEAD_DIM)
    stretch_count = lax.dynamic_index_in_dim(tok_count, stretch_id, 0, keepdims=False)
    positions = space_id * local_tok + jnp.arange(local_tok)
    keep_own = positions < stretch_count
    carry_state = (
        jnp.full((HEADS, query_span), MASKED_SCORE, jnp.float32),
        jnp.zeros((HEADS, query_span), jnp.float32),
        jnp.zeros((query_span, HEADS, HEAD_DIM), jnp.float32),
    )
    own_keys = stretch_keys.reshape(local_tok, HEADS, HEAD_DIM)
    own_values = stretch_values.reshape(local_tok, HEADS, HEAD_DIM)
    carry_state = flash_update(
        carry_state, own_keys, own_values, keep_own, every_query, score_scale
    )
    my_list = lax.dynamic_index_in_dim(block_list, stretch_id, 0, keepdims=False)
    my_len = lax.dynamic_index_in_dim(list_len, stretch_id, 0, keepdims=False)
    store_k, store_v = (
        lax.all_gather(cache_keys, "stretch", axis=0, tiled=True),
        lax.all_gather(cache_values, "stretch", axis=0, tiled=True),
    )
    groups = (my_len + PER_SRC - 1) // PER_SRC

    def visit_group(group_idx, carry_state):
        first_entry = group_idx * PER_SRC
        picked = lax.dynamic_slice_in_dim(my_list, first_entry, PER_SRC)
        piece_k = jnp.take(store_k, picked, axis=0).reshape(PER_SRC * local_tok, HEADS, HEAD_DIM)
        piece_v = jnp.take(store_v, picked, axis=0).reshape(PER_SRC * local_tok, HEADS, HEAD_DIM)
        is_live = first_entry + jnp.arange(PER_SRC) < my_len
        keep_mask = jnp.repeat(is_live, local_tok)
        return flash_update(carry_state, piece_k, piece_v, keep_mask, every_query, score_scale)

    run_max, run_sum, accumulated = lax.fori_loop(0, groups, visit_group, carry_state)
    row_top = lax.pmax(run_max.astype(jnp.bfloat16), "space").astype(run_max.dtype)
    factor = jnp.exp(run_max - row_top)
    numerator = (accumulated * jnp.transpose(factor)[:, :, None]).reshape(query_span, features)
    denominator = jnp.transpose(run_sum * factor)
    numerator, denominator = (
        lax.psum_scatter(numerator, "space", scatter_dimension=0, tiled=True),
        lax.psum_scatter(denominator, "space", scatter_dimension=0, tiled=True),
    )
    attended = numerator.reshape(local_tok, HEADS, HEAD_DIM) / denominator[:, :, None]
    mean_sq = jnp.mean(attended * attended, axis=2, keepdims=True)
    normed = attended * lax.rsqrt(mean_sq + 1e-06)
    noise_level = lax.dynamic_index_in_dim(noise_levels, stretch_id, 0, keepdims=False)
    gate_row = lax.dynamic_index_in_dim(gate_table, noise_level, 0, keepdims=False)
    result = jnp.where(
        keep_own[:, None], normed.reshape(local_tok, features) * gate_row[None, :], 0.0
    ).astype(jnp.bfloat16)
    return passed_along(result[None], "stretch", 1)


def solution(mesh):
    placed = (
        P("stretch", "space", None),
        P("stretch", "space", None),
        P("stretch", "space", None),
        P("stretch", "space", None),
        P("stretch", "space", None),
        P(),
        P(),
        P(),
        P(),
        P(),
    )
    return jax.shard_map(
        shards, mesh=mesh, in_specs=placed, out_specs=P("stretch", "space", None), check_vma=False
    )
```

profile of v0, /device:TPU:8, one launch (start us, length us, event | category | flops | bytes accessed | tf_op | source)
XLA Modules:
  0.0 1245.6 jit_solution(6136347702893729931)
XLA Ops:
  6.5 0.7 all-gather.4.cloned.1.call-update
  7.3 0.7 all-gather.6.cloned.1.call-update
  8.1 0.7 all-gather.8.cloned.1.call-update
  8.8 1.2 dynamic_slice.22
  10.6 1.3 dynamic_slice.21
  11.9 0.9 copy.44
  12.8 0.9 copy.45
  13.7 0.7 dynamic-slice_bitcast_fusion
  14.4 0.6 add_compare_fusion.1
  15.1 107.7 %all-gather.4.cloned.1.call-done = bf16[1,1024,3072]{2,1,0:T(8,128)(2,1)} async-done(((bf16[1,16,3072]{2,1,0:T(8,128)(2,1)}), bf16[1,1024,3072]{2,1,0:T(8,128)(2,1)}) %all-gather.4.cloned.1.call-update) | async-done | bytes 6291472 | tf_op jit(solution)/shard_map/all_gather | solution.py:57
  122.8 8.6 copy.30
  131.4 8.7 copy.35
  140.2 3.8 fusion.32
  144.0 0.5 fusion.17
  144.5 8.6 bitcast_add_fusion.1
  153.1 12.6 %copy.34 = f32[1024,24,128]{0,2,1:T(8,128)} copy(f32[1024,24,128]{2,0,1:T(8,128)} %bitcast_add_fusion.1) | data formatting | bytes 25165824 | tf_op jit(solution)/shard_map/while | solution.py:90
  165.7 21.1 %all-gather.6.cloned.1.call-done = bf16[32,16,3072]{2,1,0:T(8,128)(2,1)} async-done(((bf16[8,16,3072]{2,1,0:T(8,128)(2,1)}), bf16[32,16,3072]{2,1,0:T(8,128)(2,1)}) %all-gather.6.cloned.1.call-update) | async-done | bytes 3145744 | tf_op jit(solution)/shard_map/all_gather | solution.py:76
  186.9 69.2 %all-gather.8.cloned.1.call-done = bf16[32,16,3072]{2,1,0:T(8,128)(2,1)} async-done(((bf16[8,16,3072]{2,1,0:T(8,128)(2,1)}), bf16[32,16,3072]{2,1,0:T(8,128)(2,1)}) %all-gather.8.cloned.1.call-update) | async-done | bytes 3145744 | tf_op jit(solution)/shard_map/all_gather | solution.py:77
  256.0 65.4 %while.14 = (s32[]{:T(128)}, f32[24,1024]{1,0:T(8,128)S(1)}, f32[24,1024]{1,0:T(8,128)S(1)}, f32[1024,24,128]{0,2,1:T(8,128)}, s32[]{:T(128)}, /*index=5*/s32[]{...) while((s32[]{:T(128)}, f32[24,1024]{1,0:T(8,128)S(1)}, ...), condition=%wide.region_5.7_spmd, body=%wide.region_2.6_spmd.sunk | while | flops 832513024 | bytes 57414304 | solution.py:90
  256.0 0.7 compare_and_fusion.2
  256.7 2.5 gather_fusion
  259.2 2.5 gather_fusion.1
  261.6 0.1 broadcast_select_fusion.3
  261.8 0.1 broadcast_in_dim.168
  261.9 0.1 broadcast_in_dim.169
  262.0 5.1 fusion.44
  267.2 8.8 bitcast_add_fusion.3
  276.0 1.7 fusion.46
  277.7 0.1 multiply_add_fusion.2
  277.8 0.7 compare_and_fusion.2
  278.5 2.5 gather_fusion
  281.0 2.5 gather_fusion.1
  283.4 0.1 broadcast_select_fusion.3
  283.6 0.1 broadcast_in_dim.168
  283.7 0.1 broadcast_in_dim.169
  283.8 5.1 fusion.44
  289.0 8.8 bitcast_add_fusion.3
  297.8 1.7 fusion.46
  299.6 0.7 compare_and_fusion.2
  300.3 2.5 gather_fusion
  302.8 2.5 gather_fusion.1
  305.2 0.1 broadcast_select_fusion.3
  305.4 0.1 broadcast_in_dim.168
  305.5 0.1 broadcast_in_dim.169
  305.6 5.1 fusion.44
  310.8 8.8 bitcast_add_fusion.3
  319.6 1.7 fusion.46
  321.4 274.8 %pmax.7 = bf16[24,1024]{1,0:T(8,128)(2,1)S(1)} all-reduce(bf16[24,1024]{1,0:T(8,128)(2,1)S(1)} %convert_element_type.16), channel_id=1, replica_groups=mesh['stretch'=4,'space'=64] {'space'}, use_global_device_ids=true, to_apply=%region_6.8 | all-reduce | flops 24576 | bytes 98304 | tf_op jit(solution)/shard_map/pmax | solution.py:91
  596.2 12.2 broadcast_multiply_fusion
  608.4 12.6 %copy.39 = f32[1024,3072]{1,0:T(8,128)} copy(f32[1024,3072]{0,1:T(8,128)} %bitcast.74) | data formatting | bytes 25165824 | tf_op jit(solution)/shard_map/reshape | solution.py:93
  621.0 0.6 copy-done.1
  621.6 0.6 dynamic_slice.24
  624.1 1.0 copy.40
  625.2 318.2 %reduce-scatter.5.cloned.1.call-done = f32[16,3072]{1,0:T(8,128)} async-done(((f32[1024,3072]{1,0:T(8,128)}), f32[16,3072]{1,0:T(8,128)}) %reduce-scatter.5.cloned.1.call-update) | async-done | bytes 196624 | tf_op jit(solution)/shard_map/reduce_scatter | solution.py:96
  943.4 1.0 copy.47
  944.3 284.4 %reduce-scatter.7.cloned.1.call-done = f32[16,24]{1,0:T(8,128)} async-done(((f32[1024,24]{1,0:T(8,128)}), f32[16,24]{1,0:T(8,128)}) %reduce-scatter.7.cloned.1.call-update) | async-done | bytes 1552 | tf_op jit(solution)/shard_map/reduce_scatter | solution.py:97
  1228.7 0.8 bitcast_divide_fusion
  1229.6 0.1 multiply_reduce_fusion
  1229.7 0.1 mul.74
  1229.8 0.8 div.30
  1230.7 1.0 fusion.27
  1231.7 2.7 collective-permute-start
  1234.4 4.1 collective-permute-done
  1238.5 0.6 copy.88
  (33 shorter events, 0.9 us)
Async XLA Ops:
  6.5 618.6 %copy-start = (f32[48,3072]{1,0:T(8,128)S(1)}, f32[48,3072]{1,0:T(8,128)}, u32[]{:S(2)}) copy-start(f32[48,3072]{1,0:T(8,128)} %param.23) | copy-start | bytes 1769476
  6.5 116.3 %all-gather.4.cloned.1.call-start = ((), (), s32[]{:S(2)}) async-start(), calls=%async_computation.2 | async-start | bytes 6389760 | tf_op jit(solution)/shard_map/all_gather | solution.py:57
  7.3 179.6 %all-gather.6.cloned.1.call-start = ((), (), s32[]{:S(2)}) async-start(), calls=%async_computation.3 | async-start | bytes 3932160 | tf_op jit(solution)/shard_map/all_gather | solution.py:76
  8.0 248.0 %all-gather.8.cloned.1.call-start = ((), (), s32[]{:S(2)}) async-start(), calls=%async_computation.4 | async-start | bytes 3932160 | tf_op jit(solution)/shard_map/all_gather | solution.py:77
  8.7 934.6 %reduce-scatter.5.cloned.1.call-start = ((), (), s32[]{:S(2)}) async-start(), calls=%async_computation.5 | async-start | bytes 12779520 | tf_op jit(solution)/shard_map/reduce_scatter | solution.py:96
  620.9 0.7 copy-start.1
  621.0 607.8 %reduce-scatter.7.cloned.1.call-start = ((), (), s32[]{:S(2)}) async-start(), calls=%async_computation.6 | async-start | bytes 532480 | tf_op jit(solution)/shard_map/reduce_scatter | solution.py:97
  1231.7 6.8 collective-permute-start
Sparse Core Ops, SparseCore 0:
  9.2 113.5 all-gather.3
  124.6 62.1 all-gather.5
  188.7 67.3 all-gather.7
  621.1 322.2 reduce-scatter.4
  945.7 282.9 reduce-scatter.6
where the time goes:
time: 1260 us; the launch traced here: 1250 us
  waiting for transfers between devices  807 us (64%)
  blocking collectives  275 us (22%)
  local copies, waits for them, and re-layouts  67.9 us (5%)
  matrix products  54 us (4%)
  other arithmetic  23.2 us (2%)
  between operations  15.8 us (1%)
    reduce_scatter x1, waiting for transfers between devices, shards(): lax.psum_scatter(numerator, 'space', scatter_dimension=0, tiled=True)  318 us
    reduce_scatter x1, waiting for transfers between devices, shards(): lax.psum_scatter(denominator, 'space', scatter_dimension=0, tiled=True)  284 us
    pmax x1, blocking collectives, shards(): lax.pmax(run_max.astype(jnp.bfloat16), 'space').astype(run_max.dtype)  275 us
    all_gather x1, waiting for transfers between devices, shards(): gathered = lax.all_gather(queries, 'space', axis=1, tiled=True)  108 us
    all_gather x1, waiting for transfers between devices, shards(): lax.all_gather(cache_values, 'stretch', axis=0, tiled=True)  69.2 us
    dot_general x4, matrix products, flash_update(): jnp.einsum('hkq,khd->qhd', weights.astype(jnp.bfloat16), value_rows, pref...  35 us
  transfers between devices with their start and end apart: 6, of which 6 were waited for; matrix products, arithmetic and copies ran while one was open for 4% of the time, Pallas kernels for 0%

commit v1 on v0

v1 whole, which is shorter than its diff:
```python
import functools
import math

import jax
import jax.numpy as jnp
from jax import lax
from jax.experimental import pallas as pl
from jax.experimental.pallas import tpu as pltpu
from jax.sharding import Mesh
from jax.sharding import PartitionSpec as P

HEAD_DIM = 128
LOCAL_HEADS = 3
COLS = LOCAL_HEADS * HEAD_DIM
PER_SRC = 4
MEMBERS = 8
ROWS = 16
CLEAN = 8
MASKED = -1e30
UNUSED = 1e30
LOG2E = 1.4426950408889634
KEYS = 256
AXES = ("zh", "x", "yh", "yl", "zl", "core")
OFFSETS = [(dx, dy) for dx in (2, 1, 3, 0) for dy in (1, 0) if (dx, dy) != (0, 0)]


class Place:
    def __init__(self):
        for name in AXES:
            setattr(self, name, lax.axis_index(name))
        self.z = self.zh * 2 + self.zl
        self.member = self.x * 2 + self.yl

    def peer(self, dx, dy):
        return (self.x + dx) % 4, (self.yl + dy) % 2

    def to_peer(self, dx, dy):
        px, py = self.peer(dx, dy)
        return {"x": px, "yl": py}

    def to_z(self, step):
        other = (self.z + step + 8) % 8
        return {"zh": other // 2, "zl": other % 2}

    def to_y(self):
        return {"yh": 1 - self.yh}

    def to_core(self):
        return {"core": 1 - self.core}


def greet(targets):
    barrier = pltpu.get_barrier_semaphore()
    for target in targets:
        pl.semaphore_signal(barrier, inc=1, device_id=target, device_id_type=pl.DeviceIdType.MESH)
    pl.semaphore_wait(barrier, len(targets))


def remote(src, dst, send, recv, target):
    return pltpu.make_async_remote_copy(
        src_ref=src, dst_ref=dst, send_sem=send, recv_sem=recv, device_id=target, device_id_type=pl.DeviceIdType.MESH
    )


def spread_kernel(
    q, sk, sv, ck, cv, keys, values, queries, kv_send, kv_recv, q_send, q_recv, core_send, core_recv,
    up_send, up_recv, down_send, down_recv, y_send, y_recv, local,
):
    at = Place()
    greet([at.to_peer(*off) for off in OFFSETS] + [at.to_z(1), at.to_z(-1), at.to_y(), at.to_core()])

    def slot(member):
        return pl.ds(pl.multiple_of((at.core * 8 + member) * ROWS, ROWS), ROWS)

    def columns(member):
        return pl.ds(pl.multiple_of(member * COLS, COLS), COLS)

    mine = slot(at.member)
    q_row = pl.ds(pl.multiple_of(at.yh * 128 + at.member * ROWS, ROWS), ROWS)
    q_copies = []
    for n, off in enumerate(OFFSETS):
        px, py = at.peer(*off)
        copy = remote(
            q.at[0, :, columns(px * 2 + py)], queries.at[at.z, q_row, :], q_send.at[n], q_recv.at[n], at.to_peer(*off)
        )
        copy.start()
        q_copies.append(copy)
    q_own = pltpu.make_async_copy(q.at[0, :, columns(at.member)], queries.at[at.z, q_row, :], local.at[4])
    q_own.start()
    own = [
        pltpu.make_async_copy(ck.at[:, :, columns(at.member)], keys.at[pl.ds(0, CLEAN), mine, :], local.at[0]),
        pltpu.make_async_copy(cv.at[:, :, columns(at.member)], values.at[pl.ds(0, CLEAN), mine, :], local.at[1]),
        pltpu.make_async_copy(sk.at[:, :, columns(at.member)], keys.at[pl.ds(CLEAN, 1), mine, :], local.at[2]),
        pltpu.make_async_copy(sv.at[:, :, columns(at.member)], values.at[pl.ds(CLEAN, 1), mine, :], local.at[3]),
    ]
    for copy in own:
        copy.start()
    kv_copies = []
    for n, off in enumerate(OFFSETS):
        px, py = at.peer(*off)
        cols = columns(px * 2 + py)
        target = at.to_peer(*off)
        group = [
            remote(ck.at[:, :, cols], keys.at[pl.ds(0, CLEAN), mine, :], kv_send.at[n, 0], kv_recv.at[n, 0], target),
            remote(cv.at[:, :, cols], values.at[pl.ds(0, CLEAN), mine, :], kv_send.at[n, 1], kv_recv.at[n, 1], target),
            remote(sk.at[:, :, cols], keys.at[pl.ds(CLEAN, 1), mine, :], kv_send.at[n, 2], kv_recv.at[n, 2], target),
            remote(sv.at[:, :, cols], values.at[pl.ds(CLEAN, 1), mine, :], kv_send.at[n, 3], kv_recv.at[n, 3], target),
        ]
        for copy in group:
            copy.start()
        kv_copies.append(group)

    forwards = []

    def forward(n, member):
        where = slot(member)
        for part, ref in enumerate((keys, values)):
            copy = remote(
                ref.at[:, where, :], ref.at[:, where, :], core_send.at[n, part], core_recv.at[n, part], at.to_core()
            )
            copy.start()
            forwards.append(copy)

    def forward_received(n):
        for copy in kv_copies[n]:
            copy.wait_recv()
        dx, dy = OFFSETS[n]
        px, py = at.peer(-dx + 4, dy)
        forward(n, px * 2 + py)

    def half(plane, r):
        which = (at.yh + r) % 2
        return queries.at[plane, pl.ds(pl.multiple_of(which * 128, 128), 128), :]

    ring = {}

    def ring_start(up, step, r):
        plane = (at.z - step + 8) % 8 if up else (at.z + step) % 8
        send, recv = (up_send, up_recv) if up else (down_send, down_recv)
        part = half(plane, r)
        copy = remote(part, part, send.at[step, r], recv.at[step, r], at.to_z(1 if up else -1))
        copy.start()
        ring[up, step, r] = copy

    q_own.wait()
    for copy in q_copies:
        copy.wait_recv()
    y_copy = remote(half(at.z, 0), half(at.z, 0), y_send, y_recv, at.to_y())
    y_copy.start()
    ring_start(True, 0, 0)
    ring_start(False, 0, 0)
    y_copy.wait_recv()
    ring_start(True, 0, 1)
    ring_start(False, 0, 1)
    for copy in own:
        copy.wait()
    forward(7, at.member)
    order = [5, 6, 1, 3, 0, 2, 4]
    order = [n for n in range(7)][::-1]
    todo = list(order)
    for step in (1, 2, 3):
        for r in (0, 1):
            ring[True, step - 1, r].wait_recv()
            if step < 3 or r == 0:
                ring_start(True, step, r)
            ring[False, step - 1, r].wait_recv()
            if step < 3 or r == 1:
                ring_start(False, step, r)
        forward_received(todo.pop(0))
    while todo:
        forward_received(todo.pop(0))
    ring[True, 3, 0].wait_recv()
    ring[False, 3, 1].wait_recv()
    for copy in forwards:
        copy.wait_recv()
    for copy in forwards:
        copy.wait_send()
    for copy in ring.values():
        copy.wait_send()
    y_copy.wait_send()
    for copy in q_copies:
        copy.wait_send()
    for group in kv_copies:
        for copy in group:
            copy.wait_send()


def spread(q, sk, sv, ck, cv):
    hbm = pl.BlockSpec(memory_space=pl.ANY)
    dma = pltpu.SemaphoreType.DMA
    return pl.pallas_call(
        spread_kernel,
        out_shape=(
            jax.ShapeDtypeStruct((CLEAN + 1, KEYS, COLS), jnp.bfloat16),
            jax.ShapeDtypeStruct((CLEAN + 1, KEYS, COLS), jnp.bfloat16),
            jax.ShapeDtypeStruct((8, 256, COLS), jnp.bfloat16),
        ),
        in_specs=[hbm] * 5,
        out_specs=(hbm,) * 3,
        scratch_shapes=[
            dma((7, 4)), dma((7, 4)), dma((7,)), dma((7,)), dma((8, 2)), dma((8, 2)),
            dma((4, 2)), dma((4, 2)), dma((4, 2)), dma((4, 2)), dma, dma, dma((5,)),
        ],
        compiler_params=pltpu.CompilerParams(collective_id=0, has_side_effects=True),
    )(q, sk, sv, ck, cv)


def pick_blocks(block_list, list_len, stretch, owner):
    zero = jnp.int32(0)
    picked = [zero] * PER_SRC
    count = zero
    for entry in range(16):
        block = block_list[stretch, entry]
        mine = jnp.logical_and(block // CLEAN == owner, entry < list_len[stretch])
        for e in range(PER_SRC):
            picked[e] = jnp.where(jnp.logical_and(mine, count == e), block % CLEAN, picked[e])
        count = count + jnp.where(mine, 1, 0)
    return picked, count


def attend_kernel(block_list, list_len, tok_count, keys, values, queries, sums, stats, turned):
    at = Place()
    scale = LOG2E / math.sqrt(HEAD_DIM)

    def turn(block, carry):
        turned[block] = values[block].T
        return carry

    lax.fori_loop(0, CLEAN + 1, turn, 0)

    def unit(plane, carry):
        stretch = plane // 2
        dest = (plane + 2) % 8
        picked, count = pick_blocks(block_list, list_len, stretch, at.zh)

        def heads(with_own):
            def head(h, inner):
                lanes = pl.ds(pl.multiple_of(h * HEAD_DIM, HEAD_DIM), HEAD_DIM)
                q_head = queries[plane, :, lanes]
                score_parts, live, turned_parts = [], [], []
                for e in range(PER_SRC):
                    score_parts.append(
                        lax.dot_general(
                            keys[picked[e], :, lanes], q_head, (((1,), (1,)), ((), ())),
                            preferred_element_type=jnp.float32,
                        )
                    )
                    live.append(e < count)
                    turned_parts.append(turned[picked[e], lanes, :])
                if with_own:
                    own_scores = lax.dot_general(
                        keys[CLEAN, :, lanes], q_head, (((1,), (1,)), ((), ())), preferred_element_type=jnp.float32
                    )
                    j = lax.broadcasted_iota(jnp.int32, own_scores.shape, 0)
                    position = (
                        ((j // 32) % 4) * 256 + at.yh * 128 + ((j // 16) % 2) * 64 + at.zl * 32 + (j // 128) * 16 + j % 16
                    )
                    own_scores = jnp.where(position < tok_count[stretch], own_scores, MASKED)
                    score_parts.append(own_scores)
                    live.append(None)
                    turned_parts.append(turned[CLEAN, lanes, :])
                top = None
                for part, ok in zip(score_parts, live):
                    part_top = jnp.max(part, axis=0, keepdims=True)
                    if ok is not None:
                        part_top = jnp.where(ok, part_top, MASKED)
                    top = part_top if top is None else jnp.maximum(top, part_top)
                shift = top * scale
                total = None
                weight_parts = []
                for part, ok in zip(score_parts, live):
                    if ok is not None:
                        offset = jnp.where(ok, shift, UNUSED)
                    else:
                        offset = jnp.where(top > 0.5 * MASKED, shift, UNUSED)
                    weights = jnp.exp2(part * scale - offset)
                    part_total = jnp.sum(weights, axis=0, keepdims=True)
                    total = part_total if total is None else total + part_total
                    weight_parts.append(weights.astype(jnp.bfloat16))
                product = jnp.dot(
                    jnp.concatenate(turned_parts, axis=1),
                    jnp.concatenate(weight_parts, axis=0),
                    preferred_element_type=jnp.float32,
                )
                sums[dest, lanes, :] = product.astype(jnp.bfloat16)
                stats[dest, pl.ds(h, 1), :] = shift
                stats[dest, pl.ds(h + LOCAL_HEADS, 1), :] = total
                return inner

            lax.fori_loop(0, LOCAL_HEADS, head, 0)
            stats[dest, pl.ds(2 * LOCAL_HEADS, 2), :] = jnp.zeros((2, 256), jnp.float32)

        @pl.when(stretch == at.zh)
        def _():
            heads(True)

        @pl.when(stretch != at.zh)
        def _():
            heads(False)

        return carry

    lax.fori_loop(0, 8, unit, 0)


def attend(block_list, list_len, tok_count, keys, values, queries):
    smem = pl.BlockSpec(memory_space=pltpu.SMEM)
    vmem = pl.BlockSpec(memory_space=pltpu.VMEM)
    return pl.pallas_call(
        attend_kernel,
        out_shape=(
            jax.ShapeDtypeStruct((8, COLS, 256), jnp.bfloat16),
            jax.ShapeDtypeStruct((8, 8, 256), jnp.float32),
        ),
        in_specs=[smem] * 3 + [vmem] * 3,
        out_specs=(vmem, vmem),
        scratch_shapes=[pltpu.VMEM((CLEAN + 1, COLS, KEYS), jnp.bfloat16)],
        compiler_params=pltpu.CompilerParams(vmem_limit_bytes=48 * 1024 * 1024),
    )(block_list, list_len, tok_count, keys, values, queries)


def merge(parts):
    tops = [stat[0:LOCAL_HEADS] for _, stat in parts]
    top = functools.reduce(jnp.maximum, tops)
    factors = [jnp.exp2(t - top) for t in tops]
    total = functools.reduce(jnp.add, [f * stat[LOCAL_HEADS : 2 * LOCAL_HEADS] for f, (_, stat) in zip(factors, parts)])
    sums = []
    for h in range(LOCAL_HEADS):
        rows = slice(h * HEAD_DIM, (h + 1) * HEAD_DIM)
        sums.append(
            functools.reduce(
                jnp.add, [s[rows].astype(jnp.float32) * f[h : h + 1] for f, (s, _) in zip(factors, parts)]
            )
        )
    return sums, top, total


def join_kernel(
    tok_count, noise_levels, sums, stats, gate_table, out, held, held_stats, got, got_stats, y_got, y_stats, gates, ready,
    s_send, s_recv, t_send, t_recv, y_send, y_recv, out_send, out_recv, local,
):
    at = Place()
    greet([at.to_peer(*off) for off in OFFSETS] + [at.to_z(1), at.to_z(-1), at.to_y()])
    stretch = (at.zh + 3) % 4
    my_columns = pl.ds(pl.multiple_of(at.member * COLS, COLS), COLS)
    gate_copy = pltpu.make_async_copy(gate_table.at[:, my_columns], gates, local.at[0])
    gate_copy.start()
    copies = []
    for step in range(4):
        for side in (0, 1):
            dest = (at.z + 4 + step) % 8 if side == 0 else (at.z + 4 - step) % 8
            lanes = pl.ds(side * 128, 128) if step == 0 else pl.ds(0, 256)
            if step == 0:
                src, src_stats = sums.at[dest, :, lanes], stats.at[dest, :, lanes]
            else:
                copies[(step - 1) * 4 + side * 2].wait_recv()
                copies[(step - 1) * 4 + side * 2 + 1].wait_recv()
                if step == 1:
                    here = slice(side * 128, side * 128 + 128)
                    there = slice((1 - side) * 128, (1 - side) * 128 + 128)
                    held[step, side, :, there] = sums[dest, :, there]
                    held_stats[step, side, :, there] = stats[dest, :, there]
                else:
                    here = slice(0, 256)
                merged, top, total = merge(
                    [
                        (sums[dest, :, here], stats[dest, :, here]),
                        (got[step - 1, side, :, here], got_stats[step - 1, side, :, here]),
                    ]
                )
                for h in range(LOCAL_HEADS):
                    held[step, side, h * HEAD_DIM : (h + 1) * HEAD_DIM, here] = merged[h].astype(jnp.bfloat16)
                held_stats[step, side, 0:LOCAL_HEADS, here] = top
                held_stats[step, side, LOCAL_HEADS : 2 * LOCAL_HEADS, here] = total
                src, src_stats = held.at[step, side, :, lanes], held_stats.at[step, side, :, lanes]
            target = at.to_z(-1 if side == 0 else 1)
            pair = [
                remote(src, got.at[step, side, :, lanes], s_send.at[step, side], s_recv.at[step, side], target),
                remote(src_stats, got_stats.at[step, side, :, lanes], t_send.at[step, side], t_recv.at[step, side], target),
            ]
            for copy in pair:
                copy.start()
            copies += pair
    for copy in copies[-4:]:
        copy.wait_recv()

    def my_parts(lanes):
        return [
            (sums[at.z, :, lanes], stats[at.z, :, lanes]),
            (got[3, 0, :, lanes], got_stats[3, 0, :, lanes]),
            (got[3, 1, :, lanes], got_stats[3, 1, :, lanes]),
        ]

    other = pl.ds(pl.multiple_of((1 - at.yh) * 128, 128), 128)
    mine = pl.ds(pl.multiple_of(at.yh * 128, 128), 128)
    merged, top, total = merge(my_parts(other))
    for h in range(LOCAL_HEADS):
        held[0, 0, h * HEAD_DIM : (h + 1) * HEAD_DIM, 0:128] = merged[h].astype(jnp.bfloat16)
    held_stats[0, 0, 0:LOCAL_HEADS, 0:128] = top
    held_stats[0, 0, LOCAL_HEADS : 2 * LOCAL_HEADS, 0:128] = total
    y_pair = [
        remote(held.at[0, 0, :, pl.ds(0, 128)], y_got, y_send.at[0], y_recv.at[0], at.to_y()),
        remote(held_stats.at[0, 0, :, pl.ds(0, 128)], y_stats, y_send.at[1], y_recv.at[1], at.to_y()),
    ]
    for copy in y_pair:
        copy.start()
    gate_copy.wait()
    gate_row = gates[pl.ds(noise_levels[stretch], 1), :]
    r = lax.broadcasted_iota(jnp.int32, (128, HEAD_DIM), 0)
    position = (r // 32) * 256 + at.yh * 128 + ((r // 16) % 2) * 64 + at.zl * 32 + at.core * 16 + r % 16
    keep = position < tok_count[stretch]
    for copy in y_pair:
        copy.wait_recv()
    merged, top, total = merge(my_parts(mine) + [(y_got[...], y_stats[...])])
    for h in range(LOCAL_HEADS):
        attended = merged[h] / total[h : h + 1]
        mean_sq = jnp.mean(attended * attended, axis=0, keepdims=True)
        normed = (attended * lax.rsqrt(mean_sq + 1e-6)).T
        gated = jnp.where(keep, normed * gate_row[:, h * HEAD_DIM : (h + 1) * HEAD_DIM], 0.0)
        ready[:, h * HEAD_DIM : (h + 1) * HEAD_DIM] = gated.astype(jnp.bfloat16)
    outs = []
    for n, off in enumerate(OFFSETS):
        px, py = at.peer(*off)
        rows = pl.ds(pl.multiple_of((px * 2 + py) * ROWS, ROWS), ROWS)
        copy = remote(ready.at[rows, :], out.at[0, :, my_columns], out_send.at[n], out_recv.at[n], at.to_peer(*off))
        copy.start()
        outs.append(copy)
    rows = pl.ds(pl.multiple_of(at.member * ROWS, ROWS), ROWS)
    keep_copy = pltpu.make_async_copy(ready.at[rows, :], out.at[0, :, my_columns], local.at[1])
    keep_copy.start()
    for copy in copies + y_pair:
        copy.wait_send()
    keep_copy.wait()
    for copy in outs:
        copy.wait()


def join(tok_count, noise_levels, sums, stats, gate_table):
    smem = pl.BlockSpec(memory_space=pltpu.SMEM)
    vmem = pl.BlockSpec(memory_space=pltpu.VMEM)
    hbm = pl.BlockSpec(memory_space=pl.ANY)
    dma = pltpu.SemaphoreType.DMA
    return pl.pallas_call(
        join_kernel,
        out_shape=jax.ShapeDtypeStruct((1, ROWS, MEMBERS * COLS), jnp.bfloat16),
        in_specs=[smem, smem, vmem, vmem, hbm],
        out_specs=hbm,
        scratch_shapes=[
            pltpu.VMEM((4, 2, COLS, 256), jnp.bfloat16),
            pltpu.VMEM((4, 2, 8, 256), jnp.float32),
            pltpu.VMEM((4, 2, COLS, 256), jnp.bfloat16),
            pltpu.VMEM((4, 2, 8, 256), jnp.float32),
            pltpu.VMEM((COLS, 128), jnp.bfloat16),
            pltpu.VMEM((8, 128), jnp.float32),
            pltpu.VMEM((48, COLS), jnp.float32),
            pltpu.VMEM((128, COLS), jnp.bfloat16),
            dma((4, 2)), dma((4, 2)), dma((4, 2)), dma((4, 2)), dma((2,)), dma((2,)), dma((7,)), dma((7,)), dma((2,)),
        ],
        compiler_params=pltpu.CompilerParams(
            collective_id=1, has_side_effects=True, vmem_limit_bytes=48 * 1024 * 1024
        ),
    )(tok_count, noise_levels, sums, stats, gate_table)


def shards(q, sk, sv, ck, cv, block_list, list_len, tok_count, noise_levels, gate_table):
    keys, values, queries = spread(q, sk, sv, ck, cv)
    sums, stats = attend(block_list, list_len, tok_count, keys, values, queries)
    return join(tok_count, noise_levels, sums, stats, gate_table)


def solution(mesh):
    fine = Mesh(mesh.devices.reshape(4, 4, 2, 2, 2, 2), AXES)
    split = P("zh", ("x", "yh", "yl", "zl", "core"), None)
    return jax.shard_map(
        shards, mesh=fine, in_specs=(split,) * 5 + (P(),) * 5, out_specs=split, check_vma=False
    )
```

time: 1260 us -> 117 us (0.09); the launches traced: 1250 us -> 117 us
  waiting for transfers between devices: 807 us -> 0 us
  blocking collectives: 275 us -> 0 us
  Pallas kernels: 0 us -> 113 us
  local copies, waits for them, and re-layouts: 67.9 us -> 3.54 us
  matrix products: 54 us -> 0 us
  other arithmetic: 23.2 us -> 0 us
  between operations: 15.8 us -> 0.08 us
    reduce_scatter x2 -> x0, waiting for transfers between devices: 603 us -> none  [the longest x1 318 us: shards(): lax.psum_scatter(numerator, 'space', scatter_dimension=0, tiled=True)]
    pmax x1 -> x0, blocking collectives: 275 us -> none  [shards(): lax.pmax(run_max.astype(jnp.bfloat16), 'space').astype(run_max.dtype)]
    all_gather x3 -> x0, waiting for transfers between devices: 198 us -> none  [the longest x1 108 us: shards(): gathered = lax.all_gather(queries, 'space', axis=1, tiled=True)]
    pallas_call x0 -> x3, Pallas kernels: none -> 113 us  [the longest x1 51.9 us: spread(): pl.pallas_call(spread_kernel, out_shape=(jax.ShapeDtypeStruct((CLEAN + 1,...]
    dot_general x8 -> x0, matrix products: 54 us -> none  [the longest x4 35 us: flash_update(): jnp.einsum('hkq,khd->qhd', weights.astype(jnp.bfloat16), value_rows, pref...]
    while x11 -> x0, local copies, waits for them, and re-layouts: 21.7 us -> none  [the longest x2 21.3 us: shards(): lax.fori_loop(0, groups, visit_group, carry_state)]
    gather x6 -> x0, local copies, waits for them, and re-layouts: 14.8 us -> none  [the longest x3 7.38 us: visit_group(): jnp.take(store_v, picked, axis=0)]
  transfers between devices with their start and end apart: 6 -> 0, of which waited for: 6 -> 0; matrix products, arithmetic and copies ran while one was open for 4% -> 0% of each run, Pallas kernels for 0% -> 0%
where the time goes in v1:
time: 117 us
  Pallas kernels  113 us (97%)
  local copies, waits for them, and re-layouts  3.54 us (3%)
    pallas_call x1, Pallas kernels, spread(): pl.pallas_call(spread_kernel, out_shape=(jax.ShapeDtypeStruct((CLEAN + 1,...  51.9 us
    pallas_call x1, Pallas kernels, join(): pl.pallas_call(join_kernel, out_shape=jax.ShapeDtypeStruct((1, ROWS, MEMB...  37.7 us
    pallas_call x1, Pallas kernels, attend(): pl.pallas_call(attend_kernel, out_shape=(jax.ShapeDtypeStruct((8, COLS, 2...  23.4 us
    unnamed x15, local copies, waits for them, and re-layouts  3.54 us

profile of v1, /device:TPU:8, one launch (start us, length us, event | category | flops | bytes accessed | tf_op | source)
XLA Modules:
  0.0 116.7 jit_solution(5280131829776513480)
XLA Ops:
  0.0 0.0 copy-start.4
  0.0 0.0 copy-start.6
  0.0 0.0 copy-start.3
  0.0 51.9 %shard_map.100 = (bf16[9,256,384]{2,1,0:T(8,128)(2,1)}, bf16[9,256,384]{2,1,0:T(8,128)(2,1)}, bf16[8,256,384]{2,1,0:T(8,128)(2,1)}) custom-call(bf16[1,16,3072]{2,1,0:T(8,128)(2,1)} %q.1, bf16[1,16,3072]{2,1,0:T(8,128)(2,1)} %sk.1, bf16[1,16,3072]{2,1,0:T(8,128)(2,1)} %sv.1, bf16[8,16,3072]{2,1,0:T(8,128)(2,1)} %ck.1, bf16[8,16,3072]{2,1,0:T(8,128)(2,1)} %cv.1), custom_call_target="tpu_custom_call" | custom-call | tf_op jit(solution)/shard_map/pallas_call | solution.py:191
  51.9 0.0 copy-done.4
  52.0 0.0 copy-done.6
  52.0 0.0 copy-done.3
  52.0 0.0 copy-start
  52.0 1.5 %copy-done = bf16[9,256,384]{2,1,0:T(8,128)(2,1)S(1)} copy-done((bf16[9,256,384]{2,1,0:T(8,128)(2,1)S(1)}, bf16[9,256,384]{2,1,0:T(8,128)(2,1)}, u32[]{:S(2)}) %copy-start) | copy-done | bytes 1769496
  53.4 0.0 copy-start.1
  53.5 1.4 %copy-done.1 = bf16[8,256,384]{2,1,0:T(8,128)(2,1)S(1)} copy-done((bf16[8,256,384]{2,1,0:T(8,128)(2,1)S(1)}, bf16[8,256,384]{2,1,0:T(8,128)(2,1)}, u32[]{:S(2)}) %copy-start.1) | copy-done | bytes 1572888
  54.9 0.0 copy-start.2
  54.9 0.0 copy-start.5
  54.9 23.4 %shard_map.101 = (bf16[8,384,256]{2,1,0:T(8,128)(2,1)S(1)}, f32[8,8,256]{2,1,0:T(8,128)S(1)}) custom-call(s32[4,16]{1,0:T(4,128)S(1)} %copy-done.3, s32[4]{0:T(128)S(1)} %copy-done.6, s32[4]{0:T(128)S(1)} %copy-done.4, bf16[9,256,384]{2,1,0:T(8,128)(2,1)S(1)} %copy-done, bf16[9,256,384]{2,1,0:T(8,128)(2,1)} %get-tuple-element.11.values, ...), custom_call_target="tpu_custom_call" | custom-call | tf_op jit(solution)/shard_map/pallas_call | solution.py:309
  78.3 0.0 copy-done.2
  78.3 0.0 copy-done.5
  78.3 37.7 %shard_map.102 = bf16[1,16,3072]{2,1,0:T(8,128)(2,1)S(1)} custom-call(s32[4]{0:T(128)S(1)} %copy-done.4, s32[4]{0:T(128)S(1)} %copy-done.5, bf16[8,384,256]{2,1,0:T(8,128)(2,1)S(1)} %get-tuple-element.13.sums, f32[8,8,256]{2,1,0:T(8,128)S(1)} %get-tuple-element.14.stats, f32[48,3072]{1,0:T(8,128)S(1)} %copy-done.2), custom_call_target="tpu_custom_call" | custom-call | tf_op jit(solution)/shard_map/pallas_call | solution.py:443
  116.0 0.6 copy.12
Async XLA Ops:
  0.0 51.9 %copy-start.4 = (s32[4]{0:T(128)S(1)}, s32[4]{0:T(128)}, u32[]{:S(2)}) copy-start(s32[4]{0:T(128)} %tok_count.3) | copy-start | bytes 52
  0.0 52.0 %copy-start.6 = (s32[4]{0:T(128)S(1)}, s32[4]{0:T(128)}, u32[]{:S(2)}) copy-start(s32[4]{0:T(128)} %list_len.1) | copy-start | bytes 52
  0.0 52.0 %copy-start.3 = (s32[4,16]{1,0:T(4,128)S(1)}, s32[4,16]{1,0:T(4,128)}, u32[]{:S(2)}) copy-start(s32[4,16]{1,0:T(4,128)} %block_list.1) | copy-start | bytes 772
  52.0 1.5 %copy-start = (bf16[9,256,384]{2,1,0:T(8,128)(2,1)S(1)}, bf16[9,256,384]{2,1,0:T(8,128)(2,1)}, u32[]{:S(2)}) copy-start(bf16[9,256,384]{2,1,0:T(8,128)(2,1)} %get-tuple-element.10.keys) | copy-start | bytes 5308420
  53.4 1.4 %copy-start.1 = (bf16[8,256,384]{2,1,0:T(8,128)(2,1)S(1)}, bf16[8,256,384]{2,1,0:T(8,128)(2,1)}, u32[]{:S(2)}) copy-start(bf16[8,256,384]{2,1,0:T(8,128)(2,1)} %get-tuple-element.12.queries) | copy-start | bytes 4718596
  54.9 23.4 %copy-start.2 = (f32[48,3072]{1,0:T(8,128)S(1)}, f32[48,3072]{1,0:T(8,128)}, u32[]{:S(2)}) copy-start(f32[48,3072]{1,0:T(8,128)} %gate_table.1) | copy-start | bytes 1769476
  54.9 23.4 %copy-start.5 = (s32[4]{0:T(128)S(1)}, s32[4]{0:T(128)}, u32[]{:S(2)}) copy-start(s32[4]{0:T(128)} %noise_levels.1) | copy-start | bytes 52
